TPU v7x, 256 devices: a whole 4x4x8 slice. The times are simulated.
256 devices in a mesh: rep: 32 (over z_hi, x, core), fsdp: 8 (over y, z_lo).
Axes of the slice: x: 4, y: 4, z: 8 (z_hi: 4, z_lo: 2; z = z_hi * 2 + z_lo), core: 2. Of those that a mesh axis runs over, the one named last changes fastest.
Arguments:
- local_weights: bfloat16 [32, 5120, 512], P('rep', 'fsdp'), may hold values from -6 to 6
- global_weights: float32 [5120, 512], P('fsdp'), may hold values from -6 to 6
- momentum: float32 [5120, 512], P('fsdp'), may hold values from -6 to 6
- tokens: bfloat16 [131072, 5120], P(('rep', 'fsdp')), may hold values from -0.375 to 0.375
- key_grad: bfloat16 [131072, 512], P(('rep', 'fsdp')), may hold values from -6 to 6
Outputs:
- new_global: float32 [5120, 512], P('fsdp')
- new_momentum: float32 [5120, 512], P('fsdp')
- inner_keys: bfloat16 [131072, 512], P(('rep', 'fsdp'))
- weight_grad: bfloat16 [32, 5120, 512], P('rep', 'fsdp')
All inputs are finite; a program needn't handle non-finite values.
Results may differ from a plain program's by a relative error of at most 0.0049.
Values may be sent and summed in bfloat16 or wider, within the bound.
No kernel may reach another device: no remote copies, remote signals or barrier semaphores. Data moves between devices by JAX's collectives and lax.ppermute only.
A program may use at most 128 MiB of HBM per device.

v0:
```python
import jax
import jax.numpy as jnp
from jax import lax
from jax.sharding import PartitionSpec as P

momentum_rate = 0.9
outer_rate = 0.7


def per_device(local_weights, global_weights, momentum, tokens, key_grad):
    replicas = lax.axis_size("rep")
    outer_grad = global_weights - local_weights[0].astype(jnp.float32)
    summed = lax.psum(outer_grad, "rep")
    average = summed / replicas
    new_momentum = momentum_rate * momentum + average
    new_global = global_weights - outer_rate * (average + momentum_rate * new_momentum)
    start_weights = new_global.astype(jnp.bfloat16)
    columns = tokens
    inner_keys = jnp.dot(
        columns,
        lax.all_gather(start_weights, "fsdp", axis=0, tiled=True),
        preferred_element_type=jnp.float32,
    ).astype(jnp.bfloat16)
    columns = tokens
    grad_rows = lax.psum_scatter(
        lax.dot_general(
            columns, key_grad, (((0,), (0,)), ((), ())), preferred_element_type=jnp.float32
        ),
        "fsdp",
        scatter_dimension=0,
        tiled=True,
    )
    weight_grad = grad_rows.astype(jnp.bfloat16)[None]
    return (new_global, new_momentum, inner_keys, weight_grad)


def solution(mesh):
    placed = (
        P("rep", "fsdp", None),
        P("fsdp", None),
        P("fsdp", None),
        P(("rep", "fsdp"), None),
        P(("rep", "fsdp"), None),
    )
    return jax.shard_map(
        per_device,
        mesh=mesh,
        in_specs=placed,
        out_specs=(
            P("fsdp", None),
            P("fsdp", None),
            P(("rep", "fsdp"), None),
            P("rep", "fsdp", None),
        ),
        check_vma=False,
    )
```

profile of v0, /device:TPU:1, one launch (start us, length us, event | category | flops | bytes accessed | tf_op | source)
XLA Modules:
  0.0 642.0 jit_solution(12402348356338065704)
XLA Ops:
  7.2 0.0 copy-start
  7.2 0.0 all-reduce.2.cloned.1.call-start
  7.2 0.0 copy-start.2
  7.2 2.9 convert_subtract_fusion
  10.1 0.0 copy-start.1
  10.1 0.0 all-reduce.2.cloned.1.call-update
  10.1 0.0 all-gather.2.cloned.1.call-start
  10.2 293.2 %all-reduce.2.cloned.1.call-done = f32[640,512]{1,0:T(8,128)} async-done(((f32[640,512]{1,0:T(8,128)}), f32[640,512]{1,0:T(8,128)}) %all-reduce.2.cloned.1.call-update) | async-done | bytes 1310736 | tf_op jit(solution)/shard_map/psum | solution.py:13
  303.4 0.0 copy-done.2
  303.4 0.0 copy-done.1
  303.4 3.5 fusion.1
  306.9 0.0 all-gather.2.cloned.1.call-update
  306.9 0.0 reduce-scatter.2.cloned.1.call-start
  307.0 0.0 copy-done
  307.0 8.2 %fusion.2 = f32[5120,512]{1,0:T(8,128)} fusion(bf16[512,5120]{1,0:T(8,128)(2,1)} %param.8, bf16[512,512]{1,0:T(8,128)(2,1)S(1)} %copy-done), kind=kOutput, calls=%fused_computation.7 | convolution fusion | flops 2684354560 | bytes 16252928 | tf_op jit(solution)/shard_map/dot_general | solution.py:26
  315.2 0.0 reduce-scatter.2.cloned.1.call-update
  315.2 103.5 %all-gather.2.cloned.1.call-done = bf16[5120,512]{1,0:T(8,128)(2,1)} async-done(((bf16[640,512]{1,0:T(8,128)(2,1)}), bf16[5120,512]{1,0:T(8,128)(2,1)}) %all-gather.2.cloned.1.call-update) | async-done | bytes 5242896 | tf_op jit(solution)/shard_map/all_gather | solution.py:21
  418.7 7.0 %fusion = bf16[512,512]{0,1:T(8,128)(2,1)S(1)} fusion(bf16[5120,512]{1,0:T(8,128)(2,1)} %all-gather.2.cloned.1.call-done, bf16[512,5120]{1,0:T(8,128)(2,1)} %param.8), kind=kOutput, calls=%fused_computation.4 | convolution fusion | flops 2684616704 | bytes 11010048 | tf_op jit(solution)/shard_map/dot_general | solution.py:19
  425.7 1.0 copy.9
  426.7 206.6 %reduce-scatter.2.cloned.1.call-done = f32[640,512]{1,0:T(8,128)} async-done(((f32[5120,512]{1,0:T(8,128)}), f32[640,512]{1,0:T(8,128)}) %reduce-scatter.2.cloned.1.call-update) | async-done | bytes 1310736 | tf_op jit(solution)/shard_map/reduce_scatter | solution.py:25
  633.3 2.2 convert_bitcast_fusion
Async XLA Ops:
  7.2 299.8 %copy-start = (bf16[512,512]{1,0:T(8,128)(2,1)S(1)}, bf16[512,512]{1,0:T(8,128)(2,1)}, u32[]{:S(2)}) copy-start(bf16[512,512]{1,0:T(8,128)(2,1)} %param.9) | copy-start | bytes 1572868
  7.2 296.2 %all-reduce.2.cloned.1.call-start = ((), (), s32[]{:S(2)}) async-start(), calls=%async_computation.1 | async-start | bytes 2621440 | tf_op jit(solution)/shard_map/psum | solution.py:13
  7.2 296.1 %copy-start.2 = (f32[640,512]{1,0:T(8,128)S(1)}, f32[640,512]{1,0:T(8,128)}, u32[]{:S(2)}) copy-start(f32[640,512]{1,0:T(8,128)} %param.7) | copy-start | bytes 3932164
  10.1 293.3 %copy-start.1 = (f32[640,512]{1,0:T(8,128)S(1)}, f32[640,512]{1,0:T(8,128)}, u32[]{:S(2)}) copy-start(f32[640,512]{1,0:T(8,128)} %param.6) | copy-start | bytes 3932164
  10.1 408.6 %all-gather.2.cloned.1.call-start = ((), (), s32[]{:S(2)}) async-start(), calls=%async_computation.2 | async-start | bytes 5898240 | tf_op jit(solution)/shard_map/all_gather | solution.py:21
  306.9 326.3 %reduce-scatter.2.cloned.1.call-start = ((), (), s32[]{:S(2)}) async-start(), calls=%async_computation.3 | async-start | bytes 11796480 | tf_op jit(solution)/shard_map/reduce_scatter | solution.py:25
Sparse Core Ops, SparseCore 0:
  11.2 292.1 all-reduce.1
  307.1 111.5 all-gather.1
  421.4 211.8 reduce-scatter.1
where the time goes:
time: 642 us
  waiting for transfers between devices  603 us (94%)
  matrix products  15.1 us (2%)
  between operations  13.8 us (2%)
  other arithmetic  8.64 us (1%)
    psum x1, waiting for transfers between devices, per_device(): summed = lax.psum(outer_grad, 'rep')  293 us
    reduce_scatter x1, waiting for transfers between devices, per_device(): lax.psum_scatter(lax.dot_general(columns, key_grad, (((0,), (0,)), ((), (...  207 us
    all_gather x1, waiting for transfers between devices, per_device(): lax.all_gather(start_weights, 'fsdp', axis=0, tiled=True)  103 us
  transfers between devices with their start and end apart: 3, of which 3 were waited for; matrix products, arithmetic and copies ran while one was open for 3% of the time, Pallas kernels for 0%

commit v1 on v0

--- a/solution.py
+++ b/solution.py
@@ -5,6 +5,11 @@
 
 momentum_rate = 0.9
 outer_rate = 0.7
+
+
+def exchange_gather(x, axis, d):
+    sent = jnp.stack([x] * lax.axis_size(axis))
+    return jnp.concatenate(lax.all_to_all(sent, axis, 0, 0), axis=d)
 
 
 def per_device(local_weights, global_weights, momentum, tokens, key_grad):
@@ -17,9 +22,7 @@
     start_weights = new_global.astype(jnp.bfloat16)
     columns = tokens
     inner_keys = jnp.dot(
-        columns,
-        lax.all_gather(start_weights, "fsdp", axis=0, tiled=True),
-        preferred_element_type=jnp.float32,
+        columns, exchange_gather(start_weights, "fsdp", 0), preferred_element_type=jnp.float32
     ).astype(jnp.bfloat16)
     columns = tokens
     grad_rows = lax.psum_scatter(

time: 642 us -> 549 us (0.86)
  waiting for transfers between devices: 603 us -> 448 us
  blocking collectives: 0 us -> 63.6 us
    reduce_scatter x1, waiting for transfers between devices: 207 us -> 0.01 us  [per_device(): lax.psum_scatter(lax.dot_general(columns, key_grad, (((0,), (0,)), ((), (...]
    psum x1, waiting for transfers between devices: 293 us -> 448 us  [per_device(): summed = lax.psum(outer_grad, 'rep')]
    all_gather x1 -> x0, waiting for transfers between devices: 103 us -> none  [per_device(): lax.all_gather(start_weights, 'fsdp', axis=0, tiled=True)]
    all_to_all x0 -> x1, blocking collectives: none -> 63.6 us  [exchange_gather(): return jnp.concatenate(lax.all_to_all(sent, axis, 0, 0), axis=d)]
  transfers between devices with their start and end apart: 3 -> 2, of which waited for: 3 -> 1; matrix products, arithmetic and copies ran while one was open for 3% -> 3% of each run, Pallas kernels for 0% -> 0%
where the time goes in v1:
time: 549 us
  waiting for transfers between devices  448 us (82%)
  blocking collectives  63.6 us (12%)
  between operations  15.5 us (3%)
  matrix products  11.1 us (2%)
  other arithmetic  8.36 us (2%)
    psum x1, waiting for transfers between devices, per_device(): summed = lax.psum(outer_grad, 'rep')  448 us
    all_to_all x1, blocking collectives, exchange_gather(): return jnp.concatenate(lax.all_to_all(sent, axis, 0, 0), axis=d)  63.6 us
  transfers between devices with their start and end apart: 2, of which 1 were waited for; matrix products, arithmetic and copies ran while one was open for 3% of the time, Pallas kernels for 0%

profile of v1, /device:TPU:1, one launch (start us, length us, event | category | flops | bytes accessed | tf_op | source)
XLA Modules:
  0.0 548.5 jit_solution(2103154530782895190)
XLA Ops:
  8.0 0.0 copy-start
  8.0 0.0 all-reduce.2.cloned.1.call-start
  8.1 2.8 convert_subtract_fusion
  10.8 0.0 all-reduce.2.cloned.1.call-update
  10.9 0.0 reduce-scatter.2.cloned.1.call-start
  10.9 0.0 copy-done
  10.9 8.2 %fusion.2 = f32[5120,512]{1,0:T(8,128)} fusion(bf16[512,5120]{1,0:T(8,128)(2,1)} %param.8, bf16[512,512]{1,0:T(8,128)(2,1)S(1)} %copy-done), kind=kOutput, calls=%fused_computation.7 | convolution fusion | flops 2684354560 | bytes 16252928 | tf_op jit(solution)/shard_map/dot_general | solution.py:29
  19.1 0.0 copy-start.1
  19.1 0.0 copy-start.2
  19.1 0.0 reduce-scatter.2.cloned.1.call-update
  19.1 448.4 %all-reduce.2.cloned.1.call-done = f32[640,512]{1,0:T(8,128)} async-done(((f32[640,512]{1,0:T(8,128)}), f32[640,512]{1,0:T(8,128)}) %all-reduce.2.cloned.1.call-update) | async-done | bytes 1310736 | tf_op jit(solution)/shard_map/psum | solution.py:18
  467.5 0.0 copy-done.1
  467.5 0.0 copy-done.2
  467.5 3.3 fusion.1
  470.8 0.0 slice-start
  470.8 0.4 stack.2
  471.3 0.0 slice-start.1
  471.3 63.6 %all_to_all.5 = bf16[8,640,512]{2,1,0:T(8,128)(2,1)S(1)} all-to-all(bf16[8,640,512]{2,1,0:T(8,128)(2,1)S(1)} %stack.2), channel_id=1, replica_groups=mesh['rep'=32,'fsdp'=8] {'fsdp'}, dimensions={0} | all-to-all | bytes 10485760 | tf_op jit(solution)/shard_map/all_to_all | solution.py:12
  534.9 0.0 slice-done
  534.9 0.0 slice-done.1
  534.9 2.9 fusion
  537.8 1.0 copy.9
  538.8 0.0 reduce-scatter.2.cloned.1.call-done
  538.8 2.2 convert_bitcast_fusion
  (1 shorter events, 0.0 us)
Async XLA Ops:
  8.0 2.9 copy-start
  8.0 459.5 %all-reduce.2.cloned.1.call-start = ((), (), s32[]{:S(2)}) async-start(), calls=%async_computation.2 | async-start | bytes 2621440 | tf_op jit(solution)/shard_map/psum | solution.py:18
  10.9 528.0 %reduce-scatter.2.cloned.1.call-start = ((), (), s32[]{:S(2)}) async-start(), calls=%async_computation.3 | async-start | bytes 11796480 | tf_op jit(solution)/shard_map/reduce_scatter | solution.py:28
  19.1 448.4 %copy-start.1 = (f32[640,512]{1,0:T(8,128)S(1)}, f32[640,512]{1,0:T(8,128)}, u32[]{:S(2)}) copy-start(f32[640,512]{1,0:T(8,128)} %param.6) | copy-start | bytes 3932164
  19.1 448.4 %copy-start.2 = (f32[640,512]{1,0:T(8,128)S(1)}, f32[640,512]{1,0:T(8,128)}, u32[]{:S(2)}) copy-start(f32[640,512]{1,0:T(8,128)} %param.7) | copy-start | bytes 3932164
  470.8 64.1 %slice-start = ((s8[5242880]{0:T(1024)(128)(4,1)}), s8[4194304]{0:T(1024)(128)(4,1)S(1)}, s32[]{:S(2)}) async-start(s8[5242880]{0:T(1024)(128)(4,1)} %bitcast.12), calls=%async_computation.4 | async-start | bytes 8388608
  471.3 63.6 %slice-start.1 = ((s8[5242880]{0:T(1024)(128)(4,1)}), s8[1048576]{0:T(1024)(128)(4,1)S(1)}, s32[]{:S(2)}) async-start(s8[5242880]{0:T(1024)(128)(4,1)} %bitcast.12), calls=%async_computation.5 | async-start | bytes 2097152
Sparse Core Ops, SparseCore 0:
  12.0 455.4 all-reduce.1
Sparse Core Ops, SparseCore 1:
  19.2 217.1 reduce-scatter.1

commit v2 on v0

--- a/solution.py
+++ b/solution.py
@@ -10,7 +10,8 @@
 def per_device(local_weights, global_weights, momentum, tokens, key_grad):
     replicas = lax.axis_size("rep")
     outer_grad = global_weights - local_weights[0].astype(jnp.float32)
-    summed = lax.psum(outer_grad, "rep")
+    blocks = lax.all_gather(outer_grad, "rep", axis=0, tiled=False)
+    summed = blocks.sum(axis=0)
     average = summed / replicas
     new_momentum = momentum_rate * momentum + average
     new_global = global_weights - outer_rate * (average + momentum_rate * new_momentum)

time: 642 us -> 572 us (0.89)
  waiting for transfers between devices: 603 us -> 516 us
  other arithmetic: 8.64 us -> 23.9 us
    all_gather x0 -> x1, waiting for transfers between devices: none -> 378 us  [per_device(): blocks = lax.all_gather(outer_grad, 'rep', axis=0, tiled=False)]
    psum x1 -> x0, waiting for transfers between devices: 293 us -> none  [per_device(): summed = lax.psum(outer_grad, 'rep')]
    reduce_scatter x1, waiting for transfers between devices: 207 us -> 25.4 us  [per_device(): lax.psum_scatter(lax.dot_general(columns, key_grad, (((0,), (0,)), ((), (...]
    reduce_sum x0 -> x1, other arithmetic: none -> 15.3 us  [per_device(): summed = blocks.sum(axis=0)]
    all_gather x1, waiting for transfers between devices: 103 us -> 112 us  [per_device(): lax.all_gather(start_weights, 'fsdp', axis=0, tiled=True)]
  transfers between devices with their start and end apart: 3 -> 3, of which waited for: 3 -> 3; matrix products, arithmetic and copies ran while one was open for 3% -> 5% of each run, Pallas kernels for 0% -> 0%
where the time goes in v2:
time: 572 us
  waiting for transfers between devices  516 us (90%)
  other arithmetic  23.9 us (4%)
  between operations  15.5 us (3%)
  matrix products  15 us (3%)
    all_gather x1, waiting for transfers between devices, per_device(): blocks = lax.all_gather(outer_grad, 'rep', axis=0, tiled=False)  378 us
    all_gather x1, waiting for transfers between devices, per_device(): lax.all_gather(start_weights, 'fsdp', axis=0, tiled=True)  112 us
    reduce_scatter x1, waiting for transfers between devices, per_device(): lax.psum_scatter(lax.dot_general(columns, key_grad, (((0,), (0,)), ((), (...  25.4 us
    reduce_sum x1, other arithmetic, per_device(): summed = blocks.sum(axis=0)  15.3 us
  transfers between devices with their start and end apart: 3, of which 3 were waited for; matrix products, arithmetic and copies ran while one was open for 5% of the time, Pallas kernels for 0%

profile of v2, /device:TPU:1, one launch (start us, length us, event | category | flops | bytes accessed | tf_op | source)
XLA Modules:
  0.0 571.6 jit_solution(819586810412710003)
XLA Ops:
  8.0 0.0 copy-start
  8.0 0.0 all-gather.6.cloned.1.call-start
  8.1 2.8 convert_subtract_fusion
  10.8 0.0 all-gather.6.cloned.1.call-update
  10.9 0.0 reduce-scatter.2.cloned.1.call-start
  10.9 0.0 copy-done
  10.9 8.0 %fusion.2 = f32[5120,512]{1,0:T(8,128)} fusion(bf16[512,5120]{1,0:T(8,128)(2,1)} %param.8, bf16[512,512]{1,0:T(8,128)(2,1)S(1)} %copy-done), kind=kOutput, calls=%fused_computation.7 | convolution fusion | flops 2684354560 | bytes 16252928 | tf_op jit(solution)/shard_map/dot_general | solution.py:27
  18.9 0.0 reduce-scatter.2.cloned.1.call-update
  18.9 0.0 all-gather.4.cloned.1.call-start
  19.0 378.2 %all-gather.6.cloned.1.call-done = f32[20480,512]{1,0:T(8,128)} async-done(((f32[640,512]{1,0:T(8,128)}), f32[20480,512]{1,0:T(8,128)}) %all-gather.6.cloned.1.call-update) | async-done | bytes 41943056 | tf_op jit(solution)/shard_map/all_gather | solution.py:13
  397.2 0.0 copy-start.2
  397.2 15.3 %reduce_sum.9 = f32[640,512]{1,0:T(8,128)S(1)} reduce(f32[32,640,512]{2,1,0:T(8,128)} %bitcast.12, f32[]{:T(128)} %constant.1.clone.1), dimensions={0}, to_apply=%region_0.0 | reduce | flops 10158080 | bytes 43253764 | tf_op jit(solution)/shard_map/reduce_sum | solution.py:14
  412.5 0.0 copy-done.2
  412.5 3.6 fusion.1
  416.1 0.0 all-gather.4.cloned.1.call-update
  416.1 25.4 %reduce-scatter.2.cloned.1.call-done = f32[640,512]{1,0:T(8,128)} async-done(((f32[5120,512]{1,0:T(8,128)}), f32[640,512]{1,0:T(8,128)}) %reduce-scatter.2.cloned.1.call-update) | async-done | bytes 1310736 | tf_op jit(solution)/shard_map/reduce_scatter | solution.py:26
  441.5 2.2 convert_bitcast_fusion
  443.8 112.3 %all-gather.4.cloned.1.call-done = bf16[5120,512]{1,0:T(8,128)(2,1)} async-done(((bf16[640,512]{1,0:T(8,128)(2,1)}), bf16[5120,512]{1,0:T(8,128)(2,1)}) %all-gather.4.cloned.1.call-update) | async-done | bytes 5242896 | tf_op jit(solution)/shard_map/all_gather | solution.py:22
  556.1 0.0 copy-start.1
  556.1 7.0 %fusion = bf16[512,512]{0,1:T(8,128)(2,1)S(1)} fusion(bf16[5120,512]{1,0:T(8,128)(2,1)} %all-gather.4.cloned.1.call-done, bf16[512,5120]{1,0:T(8,128)(2,1)} %param.8), kind=kOutput, calls=%fused_computation.4 | convolution fusion | flops 2684616704 | bytes 11010048 | tf_op jit(solution)/shard_map/dot_general | solution.py:20
  563.1 1.0 copy.9
  564.2 0.0 copy-done.1
Async XLA Ops:
  8.0 2.9 copy-start
  8.0 389.2 %all-gather.6.cloned.1.call-start = ((), (), s32[]{:S(2)}) async-start(), calls=%async_computation.3 | async-start | bytes 43253760 | tf_op jit(solution)/shard_map/all_gather | solution.py:13
  10.9 430.7 %reduce-scatter.2.cloned.1.call-start = ((), (), s32[]{:S(2)}) async-start(), calls=%async_computation.2 | async-start | bytes 11796480 | tf_op jit(solution)/shard_map/reduce_scatter | solution.py:26
  18.9 537.2 %all-gather.4.cloned.1.call-start = ((), (), s32[]{:S(2)}) async-start(), calls=%async_computation.1 | async-start | bytes 5898240 | tf_op jit(solution)/shard_map/all_gather | solution.py:22
  397.2 15.3 %copy-start.2 = (f32[640,512]{1,0:T(8,128)S(1)}, f32[640,512]{1,0:T(8,128)}, u32[]{:S(2)}) copy-start(f32[640,512]{1,0:T(8,128)} %param.6) | copy-start | bytes 3932164
  556.1 8.0 %copy-start.1 = (bf16[512,512]{1,0:T(8,128)(2,1)S(1)}, bf16[512,512]{1,0:T(8,128)(2,1)}, u32[]{:S(2)}) copy-start(bf16[512,512]{1,0:T(8,128)(2,1)} %param.9) | copy-start | bytes 1572868
Sparse Core Ops, SparseCore 0:
  12.0 385.1 all-gather.5
Sparse Core Ops, SparseCore 1:
  19.0 422.5 reduce-scatter.1
  443.2 112.9 all-gather.3
